TPU v7x, 32 devices: a whole 2x2x4 slice. The times are simulated.
32 devices in a mesh: groups: 2 (over y), gx: 8 (over z, x), yz: 2 (over core).
Axes of the slice: x: 2, y: 2, z: 4, core: 2. Of those that a mesh axis runs over, the one named last changes fastest.
Arguments:
- tokens: bfloat16 [64, 18432], P(('groups', 'gx'), 'yz'), parts along dimension 0, may hold values from -80 to 80
- w_query: bfloat16 [18432, 6144], P('yz', 'gx'), may hold values from -0.046875 to 0.046875
- w_keyval: bfloat16 [18432, 512], P('yz', 'gx'), may hold values from -0.046875 to 0.046875
- w_inner: bfloat16 [18432, 9216], P('yz', 'gx'), may hold values from -0.046875 to 0.046875
- w_outer: bfloat16 [9216, 18432], P('gx', 'yz'), may hold values from -0.0625 to 0.0625
- w_attn_out: bfloat16 [6144, 18432], P('gx', 'yz'), may hold values from -0.4375 to 0.4375
- key_cache: bfloat16 [64, 2048, 256], P(('groups', 'gx', 'yz')), parts along dimension 0, may hold values from -1300 to 1300
- value_cache: bfloat16 [64, 2048, 256], P(('groups', 'gx', 'yz')), parts along dimension 0, may hold values from -6 to 6
- lengths: int32 [64], P(('groups', 'gx', 'yz')), parts along dimension 0, may hold values from 2 to 2048, as said below
Outputs:
- mixed: bfloat16 [64, 18432], P(('groups', 'gx'), 'yz'), parts along dimension 0
There are 2 independent parts, one for each index of `groups`. A program takes and returns all parts, laid end to end along the dimension named above; an argument that names none is the same for every part. Nothing has to cross between parts.
Inputs may be any that keep to these rules, and one draw needn't show every extreme that they name: `lengths`: each request has at least two cached positions; some request in every draw has all 2048.
All inputs are finite; a program needn't handle non-finite values.
Results may differ from a plain program's by a relative error of at most 0.006.
The roundings to bfloat16 on the way count: a program that leaves them out, or rounds other values in their place, can miss the bound.
Values may be sent and summed in bfloat16 or wider, within the bound.
A program may use at most 192 MiB of HBM per device.

v0:
```python
import jax
import jax.numpy as jnp
from jax import lax
from jax.sharding import PartitionSpec as P

D = 18432
HEAD = 256


def attend_block(query, key_cache, value_cache, lengths, new_key, new_value):
    scale = 1.0 / HEAD**0.5
    scores = (
        jnp.einsum("rhd,rsd->rhs", query, key_cache, preferred_element_type=jnp.float32) * scale
    )
    positions = lax.broadcasted_iota(jnp.int32, (1, 1, key_cache.shape[1]), 2)
    valid = positions < lengths[:, None, None]
    self_score = (
        jnp.einsum("rhd,rd->rh", query, new_key, preferred_element_type=jnp.float32) * scale
    )
    masked = jnp.where(valid, scores, -jnp.inf)
    top = jnp.maximum(jnp.max(masked, axis=2), self_score)
    cached = jnp.where(valid, jnp.exp(masked - top[:, :, None]), 0.0)
    own = jnp.exp(self_score - top)
    total = jnp.sum(cached, axis=2) + own
    cached_w = (cached / total[:, :, None]).astype(jnp.bfloat16)
    own_w = (own / total).astype(jnp.bfloat16)
    result = jnp.einsum("rhs,rsd->rhd", cached_w, value_cache, preferred_element_type=jnp.float32)
    result = (
        result + own_w.astype(jnp.float32)[:, :, None] * new_value.astype(jnp.float32)[:, None, :]
    )
    return result.astype(jnp.bfloat16).reshape(query.shape[0], query.shape[1] * query.shape[2])


def body(tokens, w_query, w_keyval, w_inner, w_outer, w_attn_out, key_cache, value_cache, lengths):
    x = tokens.astype(jnp.float32)
    moment_one, moment_two = lax.psum((jnp.sum(x, axis=1), jnp.sum(x * x, axis=1)), "yz")
    mean = moment_one / D
    var = moment_two / D - mean * mean
    normed_local = ((x - mean[:, None]) * lax.rsqrt(var + 1e-05)[:, None]).astype(jnp.bfloat16)
    normed = lax.all_gather(normed_local, "gx", axis=0, tiled=True)
    query_part = jnp.dot(normed, w_query, preferred_element_type=jnp.float32)
    keyval_part = jnp.dot(normed, w_keyval, preferred_element_type=jnp.float32)
    query_rows, keyval_rows = (
        lax.all_to_all(query_part, "gx", split_axis=0, concat_axis=1, tiled=True),
        lax.all_to_all(keyval_part, "gx", split_axis=0, concat_axis=1, tiled=True),
    )
    query_sum, keyval_sum = (
        lax.psum_scatter(query_rows, "yz", scatter_dimension=0, tiled=True),
        lax.psum_scatter(keyval_rows, "yz", scatter_dimension=0, tiled=True),
    )
    inner_part = jnp.dot(normed, w_inner, preferred_element_type=jnp.float32)
    inner_total = lax.psum(inner_part.astype(jnp.bfloat16), "yz").astype(jnp.float32)
    hidden = jax.nn.gelu(inner_total, approximate=True).astype(jnp.bfloat16)
    local_rows = query_sum.shape[0]
    query = query_sum.astype(jnp.bfloat16).reshape(local_rows, query_sum.shape[1] // HEAD, HEAD)
    keyval = keyval_sum.astype(jnp.bfloat16)
    attended = attend_block(
        query, key_cache, value_cache, lengths, keyval[:, :HEAD], keyval[:, HEAD:]
    )
    paired_rows = lax.all_gather(attended, "yz", axis=0, tiled=True)
    attended_cols = lax.all_to_all(paired_rows, "gx", split_axis=1, concat_axis=0, tiled=True)
    branch = lax.psum_scatter(
        jnp.dot(attended_cols, w_attn_out, preferred_element_type=jnp.float32)
        + jnp.dot(hidden, w_outer, preferred_element_type=jnp.float32),
        "gx",
        scatter_dimension=0,
        tiled=True,
    )
    return (x + branch).astype(jnp.bfloat16)


def solution(mesh):
    in_specs = (
        P(("groups", "gx"), "yz"),
        P("yz", "gx"),
        P("yz", "gx"),
        P("yz", "gx"),
        P("gx", "yz"),
        P("gx", "yz"),
        P(("groups", "gx", "yz"), None, None),
        P(("groups", "gx", "yz"), None, None),
        P(("groups", "gx", "yz")),
    )
    out_specs = P(("groups", "gx"), "yz")
    return jax.shard_map(body, mesh=mesh, in_specs=in_specs, out_specs=out_specs, check_vma=False)
```

profile of v0, /device:TPU:0, one launch (start us, length us, event | category | flops | bytes accessed | tf_op | source)
XLA Modules:
  0.0 216.2 jit_solution(11450761783432870110)
XLA Ops:
  6.5 0.0 copy-start
  6.5 1.2 convert_reduce_fusion
  7.8 2.6 %all-reduce.4 = (f32[4]{0:T(128)S(1)}, f32[4]{0:T(128)S(1)}) all-reduce(f32[4]{0:T(128)S(1)} %get-tuple-element.6, f32[4]{0:T(128)S(1)} %get-tuple-element.5), channel_id=1, replica_groups=mesh['groups'=2,'gx'=8,'yz'=2] {'yz'}, use_global_device_ids=true, to_apply=%region_3.0 | all-reduce | flops 8 | bytes 64 | tf_op jit(solution)/shard_map/psum | solution.py:36
  10.4 1.0 fusion.18
  11.4 33.2 %all-gather = bf16[8,4,9216]{2,1,0:T(4,128)(2,1)S(1)} all-gather(bf16[1,4,9216]{2,1,0:T(4,128)(2,1)S(1)} %fusion.18), channel_id=1, replica_groups=mesh['groups'=2,'gx'=8,'yz'=2] {'gx'}, dimensions={0}, use_global_device_ids=true | all-gather | bytes 663552 | tf_op jit(solution)/shard_map/all_gather | solution.py:40
  44.6 0.1 reshape.45
  44.7 1.7 fusion.38
  46.4 0.7 reshape.55
  47.1 5.5 %all-to-all-start.1 = ((f32[8,1,256]{2,1,0:T(1,128)}), f32[8,1,256]{2,1,0:T(1,128)S(1)}, u32[]{:S(2)}, u32[]{:S(2)}) async-start(f32[8,1,256]{2,1,0:T(1,128)} %reshape.55), calls=%async_computation.1 | async-start | bytes 16384 | tf_op jit(solution)/shard_map/all_to_all | solution.py:45
  52.6 0.0 copy-start.3
  52.6 0.0 copy-start.6
  52.6 7.5 %fusion.37 = f32[32,768]{1,0:T(8,128)S(1)} fusion(bf16[32,9216]{1,0:T(8,128)(2,1)S(1)} %reshape.45, bf16[9216,768]{1,0:T(8,128)(2,1)} %param.10), kind=kOutput, calls=%fused_computation.60 | convolution fusion | flops 452984832 | bytes 14843904 | tf_op jit(solution)/shard_map/dot_general | solution.py:41
  60.1 0.7 all_to_all.42
  60.8 0.0 all-to-all-done.1
  60.8 6.0 %all-to-all-start = ((f32[8,4,768]{2,1,0:T(4,128)}), f32[8,4,768]{2,1,0:T(4,128)S(1)}, u32[]{:S(2)}, u32[]{:S(2)}) async-start(f32[8,4,768]{2,1,0:T(4,128)} %all_to_all.42), calls=%async_computation | async-start | bytes 196608 | tf_op jit(solution)/shard_map/all_to_all | solution.py:44
  66.8 0.0 copy-done.3
  66.8 0.1 iota_compare_fusion
  66.9 0.0 copy-done.6
  66.9 0.6 dynamic-slice
  68.1 0.5 broadcast.34
  68.6 0.7 reduce
  69.3 0.1 reshape.56
  69.4 0.1 all_to_all.49
  69.5 4.4 %all-to-all-done = f32[8,4,768]{2,1,0:T(4,128)S(1)} async-done(((f32[8,4,768]{2,1,0:T(4,128)}), f32[8,4,768]{2,1,0:T(4,128)S(1)}, u32[]{:S(2)}, u32[]{:S(2)}) %all-to-all-start) | async-done | bytes 98336 | tf_op jit(solution)/shard_map/all_to_all | solution.py:44
  73.9 3.7 %all-reduce.3 = (bf16[4,6144]{1,0:T(4,128)(2,1)S(1)}, bf16[4,512]{1,0:T(4,128)(2,1)S(1)}) all-reduce(f32[4,6144]{1,0:T(4,128)S(1)} %bitcast.33, f32[4,512]{1,0:T(4,128)S(1)} %all_to_all.49), channel_id=2, replica_groups=mesh['groups'=2,'gx'=8,'yz'=2] {'yz'}, use_global_device_ids=true, to_apply=%region_4.0.clone | all-reduce | flops 26624 | bytes 159744
  77.6 0.0 copy-start.4
  77.7 0.1 fusion.23
  77.8 0.0 copy-done
  77.8 0.8 fusion.36
  78.6 0.2 fusion.2
  78.8 0.4 copy-done.4
  79.2 0.5 fusion.1
  79.7 1.8 all-gather.1
  81.6 0.6 copy.14
  82.2 3.3 %all-to-all-start.2 = ((bf16[4,8,768]{2,0,1:T(4,128)(2,1)}), bf16[4,8,768]{2,0,1:T(4,128)(2,1)S(1)}, u32[]{:S(2)}, u32[]{:S(2)}) async-start(bf16[4,8,768]{2,0,1:T(4,128)(2,1)} %copy.14), calls=%async_computation.2 | async-start | bytes 98304 | tf_op jit(solution)/shard_map/all_to_all | solution.py:61
  85.6 0.0 all-reduce.8.cloned.1.call-start
  85.6 9.5 %convolution_convert_fusion = bf16[32,1152]{1,0:T(8,128)(2,1)} fusion(bf16[32,9216]{1,0:T(8,128)(2,1)S(1)} %reshape.45, bf16[9216,1152]{1,0:T(8,128)(2,1)} %param.12), kind=kOutput, calls=%fused_computation.3 | convolution fusion | flops 679514112 | bytes 21897216 | tf_op jit(solution)/shard_map/dot_general | solution.py:51
  95.1 0.0 all-reduce.8.cloned.1.call-update
  95.2 0.0 all-reduce.10.cloned.1.call-start
  95.2 0.0 all-to-all-done.2
  95.2 7.5 %fusion.39 = f32[32,9216]{1,0:T(8,128)S(1)} fusion(bf16[32,768]{1,0:T(8,128)(2,1)S(1)} %all_to_all.53, bf16[768,9216]{1,0:T(8,128)(2,1)} %param.14), kind=kOutput, calls=%fused_computation.62 | convolution fusion | flops 452984832 | bytes 15384576 | tf_op jit(solution)/shard_map/dot_general | solution.py:63
  102.8 0.0 copy-start.5
  102.8 0.0 copy-start.2
  102.8 11.5 %all-reduce.8.cloned.1.call-done = bf16[32,1152]{1,0:T(8,128)(2,1)} async-done(((bf16[32,1152]{1,0:T(8,128)(2,1)}), bf16[32,1152]{1,0:T(8,128)(2,1)}) %all-reduce.8.cloned.1.call-update) | async-done | bytes 73744 | tf_op jit(solution)/shard_map/psum | solution.py:52
  114.3 0.0 copy-start.1
  114.3 12.0 %convolution_add_fusion = f32[32,9216]{1,0:T(8,128)} fusion(f32[32,9216]{1,0:T(8,128)S(1)} %fusion.39, bf16[1152,9216]{1,0:T(8,128)(2,1)} %param.13, bf16[32,1152]{1,0:T(8,128)(2,1)} %all-reduce.8.cloned.1.call-done), kind=kOutput, calls=%fused_computation | convolution fusion | flops 680140800 | bytes 23666688 | tf_op jit(solution)/shard_map/dot_general | solution.py:64
  126.3 0.0 all-reduce.10.cloned.1.call-update
  126.3 0.0 copy-done.5
  126.3 0.6 dynamic-slice.4
  127.5 80.2 %all-reduce.10.cloned.1.call-done = f32[32,9216]{1,0:T(8,128)} async-done(((f32[32,9216]{1,0:T(8,128)}), f32[32,9216]{1,0:T(8,128)}) %all-reduce.10.cloned.1.call-update) | async-done | bytes 1179664
  207.8 0.0 copy-done.2
  207.8 1.6 fusion.10
  209.4 0.0 copy-done.1
  (10 shorter events, 0.2 us)
Async XLA Ops:
  6.5 71.3 %copy-start = (bf16[2,2048,256]{2,1,0:T(8,128)(2,1)S(1)}, bf16[2,2048,256]{2,1,0:T(8,128)(2,1)}, u32[]{:S(2)}) copy-start(bf16[2,2048,256]{2,1,0:T(8,128)(2,1)} %param.15) | copy-start | bytes 6291460
  47.1 13.6 %all-to-all-start.1 = ((f32[8,1,256]{2,1,0:T(1,128)}), f32[8,1,256]{2,1,0:T(1,128)S(1)}, u32[]{:S(2)}, u32[]{:S(2)}) async-start(f32[8,1,256]{2,1,0:T(1,128)} %reshape.55), calls=%async_computation.1 | async-start | bytes 16384 | tf_op jit(solution)/shard_map/all_to_all | solution.py:45
  52.6 14.2 %copy-start.3 = (s32[2]{0:T(128)S(1)}, s32[2]{0:T(128)}, u32[]{:S(2)}) copy-start(s32[2]{0:T(128)} %param.17) | copy-start | bytes 28
  52.6 14.3 %copy-start.6 = (u32[32]{0:T(128)S(1)}, u32[32]{0:T(128)}, u32[]{:S(2)}) copy-start(u32[32]{0:T(128)} %constant.27) | copy-start | bytes 388
  60.8 13.1 %all-to-all-start = ((f32[8,4,768]{2,1,0:T(4,128)}), f32[8,4,768]{2,1,0:T(4,128)S(1)}, u32[]{:S(2)}, u32[]{:S(2)}) async-start(f32[8,4,768]{2,1,0:T(4,128)} %all_to_all.42), calls=%async_computation | async-start | bytes 196608 | tf_op jit(solution)/shard_map/all_to_all | solution.py:44
  77.6 1.6 copy-start.4
  82.2 13.0 %all-to-all-start.2 = ((bf16[4,8,768]{2,0,1:T(4,128)(2,1)}), bf16[4,8,768]{2,0,1:T(4,128)(2,1)S(1)}, u32[]{:S(2)}, u32[]{:S(2)}) async-start(bf16[4,8,768]{2,0,1:T(4,128)(2,1)} %copy.14), calls=%async_computation.2 | async-start | bytes 98304 | tf_op jit(solution)/shard_map/all_to_all | solution.py:61
  85.6 28.7 %all-reduce.8.cloned.1.call-start = ((), (), s32[]{:S(2)}) async-start(), calls=%async_computation.3 | async-start | bytes 147456 | tf_op jit(solution)/shard_map/psum | solution.py:52
  95.2 112.6 %all-reduce.10.cloned.1.call-start = ((), (), s32[]{:S(2)}) async-start(), calls=%async_computation.4 | async-start | bytes 2359296
  102.8 23.5 %copy-start.5 = (u32[32]{0:T(128)S(1)}, u32[32]{0:T(128)}, u32[]{:S(2)}) copy-start(u32[32]{0:T(128)} %constant.35) | copy-start | bytes 388
  102.8 105.0 %copy-start.2 = (bf16[4,9216]{1,0:T(4,128)(2,1)S(1)}, bf16[4,9216]{1,0:T(4,128)(2,1)}, u32[]{:S(2)}) copy-start(bf16[4,9216]{1,0:T(4,128)(2,1)} %param.9) | copy-start | bytes 221188
  114.3 95.1 %copy-start.1 = (bf16[2,2048,256]{2,1,0:T(8,128)(2,1)S(1)}, bf16[2,2048,256]{2,1,0:T(8,128)(2,1)}, u32[]{:S(2)}) copy-start(bf16[2,2048,256]{2,1,0:T(8,128)(2,1)} %param.15) | copy-start | bytes 6291460
Sparse Core Ops, SparseCore 0:
  95.3 18.9 all-reduce.7
  126.4 81.3 all-reduce.9
where the time goes:
time: 217 us; the launch traced here: 216 us
  waiting for transfers between devices  96.2 us (44%)
  blocking collectives  41.4 us (19%)
  matrix products  39.5 us (18%)
  starting transfers between devices  14.9 us (7%)
  between operations  14.9 us (7%)
  other arithmetic  4.89 us (2%)
  local copies, waits for them, and re-layouts  4.53 us (2%)
    unnamed x3, waiting for transfers between devices  80.3 us
    all_gather x1, blocking collectives, body(): normed = lax.all_gather(normed_local, 'gx', axis=0, tiled=True)  33.2 us
    dot_general x1, matrix products, body(): jnp.dot(hidden, w_outer, preferred_element_type=jnp.float32)  12 us
    psum x1, waiting for transfers between devices, body(): lax.psum(inner_part.astype(jnp.bfloat16), 'yz').astype(jnp.float32)  11.5 us
    dot_general x1, matrix products, body(): inner_part = jnp.dot(normed, w_inner, preferred_element_type=jnp.float32)  9.49 us
    dot_general x1, matrix products, body(): jnp.dot(attended_cols, w_attn_out, preferred_element_type=jnp.float32)  7.55 us
    dot_general x1, matrix products, body(): query_part = jnp.dot(normed, w_query, preferred_element_type=jnp.float32)  7.48 us
    all_to_all x1, starting transfers between devices, body(): lax.all_to_all(query_part, 'gx', split_axis=0, concat_axis=1, tiled=True)  6 us
  transfers between devices with their start and end apart: 5, of which 3 were waited for; matrix products, arithmetic and copies ran while one was open for 13% of the time, Pallas kernels for 0%

commit v1 on v0

--- a/solution.py
+++ b/solution.py
@@ -37,7 +37,11 @@
     mean = moment_one / D
     var = moment_two / D - mean * mean
     normed_local = ((x - mean[:, None]) * lax.rsqrt(var + 1e-05)[:, None]).astype(jnp.bfloat16)
-    normed = lax.all_gather(normed_local, "gx", axis=0, tiled=True)
+    n = lax.axis_size("gx")
+    copies = jnp.broadcast_to(normed_local[None], (n,) + normed_local.shape)
+    normed = lax.all_to_all(copies, "gx", split_axis=0, concat_axis=0, tiled=True).reshape(
+        n * normed_local.shape[0], normed_local.shape[1]
+    )
     query_part = jnp.dot(normed, w_query, preferred_element_type=jnp.float32)
     keyval_part = jnp.dot(normed, w_keyval, preferred_element_type=jnp.float32)
     query_rows, keyval_rows = (
@@ -49,7 +53,7 @@
         lax.psum_scatter(keyval_rows, "yz", scatter_dimension=0, tiled=True),
     )
     inner_part = jnp.dot(normed, w_inner, preferred_element_type=jnp.float32)
-    inner_total = lax.psum(inner_part.astype(jnp.bfloat16), "yz").astype(jnp.float32)
+    inner_total = inner_part + lax.ppermute(inner_part, "yz", [(0, 1), (1, 0)])
     hidden = jax.nn.gelu(inner_total, approximate=True).astype(jnp.bfloat16)
     local_rows = query_sum.shape[0]
     query = query_sum.astype(jnp.bfloat16).reshape(local_rows, query_sum.shape[1] // HEAD, HEAD)
@@ -59,13 +63,12 @@
     )
     paired_rows = lax.all_gather(attended, "yz", axis=0, tiled=True)
     attended_cols = lax.all_to_all(paired_rows, "gx", split_axis=1, concat_axis=0, tiled=True)
-    branch = lax.psum_scatter(
-        jnp.dot(attended_cols, w_attn_out, preferred_element_type=jnp.float32)
-        + jnp.dot(hidden, w_outer, preferred_element_type=jnp.float32),
-        "gx",
-        scatter_dimension=0,
-        tiled=True,
+    part = jnp.dot(attended_cols, w_attn_out, preferred_element_type=jnp.float32) + jnp.dot(
+        hidden, w_outer, preferred_element_type=jnp.float32
     )
+    pieces = part.astype(jnp.bfloat16).reshape(n, x.shape[0], x.shape[1])
+    pieces = lax.all_to_all(pieces, "gx", split_axis=0, concat_axis=0, tiled=True)
+    branch = jnp.sum(pieces.astype(jnp.float32), axis=0)
     return (x + branch).astype(jnp.bfloat16)
 
 

time: 217 us -> 120 us (0.55)
  waiting for transfers between devices: 96.2 us -> 4.3 us
  between operations: 14.9 us -> 0.86 us
  blocking collectives: 41.4 us -> 54.5 us
    unnamed x3 -> x0, waiting for transfers between devices: 80.3 us -> none
    all_to_all x0 -> x2, blocking collectives: none -> 46.4 us  [the longest x1 23.8 us: body(): lax.all_to_all(copies, 'gx', split_axis=0, concat_axis=0, tiled=True)]
    all_gather x1 -> x0, blocking collectives: 33.2 us -> none  [body(): normed = lax.all_gather(normed_local, 'gx', axis=0, tiled=True)]
    psum x1 -> x0, waiting for transfers between devices: 11.5 us -> none  [body(): lax.psum(inner_part.astype(jnp.bfloat16), 'yz').astype(jnp.float32)]
  transfers between devices with their start and end apart: 5 -> 4, of which waited for: 3 -> 1; matrix products, arithmetic and copies ran while one was open for 13% -> 22% of each run, Pallas kernels for 0% -> 0%
where the time goes in v1:
time: 120 us; the launch traced here: 119 us
  blocking collectives  54.5 us (45%)
  matrix products  38.5 us (32%)
  starting transfers between devices  13 us (11%)
  waiting for transfers between devices  4.3 us (4%)
  other arithmetic  4.17 us (3%)
  local copies, waits for them, and re-layouts  3.63 us (3%)
    all_to_all x1, blocking collectives, body(): lax.all_to_all(copies, 'gx', split_axis=0, concat_axis=0, tiled=True)  23.8 us
    all_to_all x1, blocking collectives, body(): lax.all_to_all(pieces, 'gx', split_axis=0, concat_axis=0, tiled=True)  22.6 us
    dot_general x1, matrix products, body(): jnp.dot(hidden, w_outer, preferred_element_type=jnp.float32)  10.9 us
    dot_general x1, matrix products, body(): inner_part = jnp.dot(normed, w_inner, preferred_element_type=jnp.float32)  8.87 us
    dot_general x1, matrix products, body(): query_part = jnp.dot(normed, w_query, preferred_element_type=jnp.float32)  8.04 us
    dot_general x1, matrix products, body(): jnp.dot(attended_cols, w_attn_out, preferred_element_type=jnp.float32)  7.55 us
    all_to_all x1, starting transfers between devices, body(): lax.all_to_all(query_part, 'gx', split_axis=0, concat_axis=1, tiled=True)  5.93 us
    all_to_all x1, waiting for transfers between devices, body(): lax.all_to_all(query_part, 'gx', split_axis=0, concat_axis=1, tiled=True)  4.29 us
  transfers between devices with their start and end apart: 4, of which 1 were waited for; matrix products, arithmetic and copies ran while one was open for 22% of the time, Pallas kernels for 0%

profile of v1, /device:TPU:0, one launch (start us, length us, event | category | flops | bytes accessed | tf_op | source)
XLA Modules:
  0.0 119.0 jit_solution(15060229830117573430)
XLA Ops:
  0.0 0.0 copy-start
  0.0 1.2 %convert_reduce_fusion.1 = (f32[4]{0:T(128)S(1)}, f32[4]{0:T(128)S(1)}) fusion(bf16[4,9216]{1,0:T(4,128)(2,1)} %param.9), kind=kLoop, calls=%fused_computation.17 | loop fusion | flops 147448 | bytes 73760 | tf_op jit(solution)/shard_map/reduce_sum | solution.py:36
  1.3 2.6 %all-reduce.3 = (f32[4]{0:T(128)S(1)}, f32[4]{0:T(128)S(1)}) all-reduce(f32[4]{0:T(128)S(1)} %get-tuple-element.6, f32[4]{0:T(128)S(1)} %get-tuple-element.5), channel_id=1, replica_groups=mesh['groups'=2,'gx'=8,'yz'=2] {'yz'}, use_global_device_ids=true, to_apply=%region_3.0 | all-reduce | flops 8 | bytes 64 | tf_op jit(solution)/shard_map/psum | solution.py:36
  3.9 1.0 fusion.21
  4.8 0.2 broadcast_in_dim.32
  5.0 23.8 %all_to_all.61 = bf16[8,4,9216]{2,1,0:T(4,128)(2,1)S(1)} all-to-all(bf16[8,4,9216]{2,1,0:T(4,128)(2,1)S(1)} %broadcast_in_dim.32), channel_id=1, replica_groups=mesh['groups'=2,'gx'=8,'yz'=2] {'gx'}, dimensions={0} | all-to-all | bytes 1179648 | tf_op jit(solution)/shard_map/all_to_all | solution.py:42
  28.8 1.8 %fusion.4 = f32[8,4,64]{2,1,0:T(4,128)S(1)} fusion(bf16[8,4,9216]{2,1,0:T(4,128)(2,1)S(1)} %all_to_all.61, bf16[9216,64]{0,1:T(8,128)(2,1)} %param.11), kind=kOutput, calls=%fused_computation.6 | convolution fusion | flops 37748736 | bytes 1777664 | tf_op jit(solution)/shard_map/dot_general | solution.py:46
  30.6 0.7 reshape.67
  31.3 3.3 %all-to-all-start.2 = ((f32[8,1,256]{2,1,0:T(1,128)}), f32[8,1,256]{2,1,0:T(1,128)S(1)}, u32[]{:S(2)}, u32[]{:S(2)}) async-start(f32[8,1,256]{2,1,0:T(1,128)} %reshape.67), calls=%async_computation.2 | async-start | bytes 16384 | tf_op jit(solution)/shard_map/all_to_all | solution.py:49
  34.6 0.0 copy-start.3
  34.6 0.0 copy-start.5
  34.6 8.0 %fusion = f32[8,4,768]{2,1,0:T(4,128)} fusion(bf16[8,4,9216]{2,1,0:T(4,128)(2,1)S(1)} %all_to_all.61, bf16[9216,768]{1,0:T(8,128)(2,1)} %param.10), kind=kOutput, calls=%fused_computation | convolution fusion | flops 452984832 | bytes 14843904 | tf_op jit(solution)/shard_map/dot_general | solution.py:45
  42.7 0.0 all-to-all-done.2
  42.7 5.9 %all-to-all-start.1 = ((f32[8,4,768]{2,1,0:T(4,128)}), f32[8,4,768]{2,1,0:T(4,128)S(1)}, u32[]{:S(2)}, u32[]{:S(2)}) async-start(f32[8,4,768]{2,1,0:T(4,128)} %fusion), calls=%async_computation.1 | async-start | bytes 196608 | tf_op jit(solution)/shard_map/all_to_all | solution.py:48
  48.6 0.0 copy-done.3
  48.6 0.1 iota_compare_fusion
  48.7 0.0 copy-done.5
  48.7 0.6 dynamic-slice
  50.0 0.1 reshape.55
  50.1 0.5 broadcast.35
  50.6 0.7 reduce
  51.3 0.1 reshape.68
  51.4 0.1 all_to_all.50
  51.5 4.3 %all-to-all-done.1 = f32[8,4,768]{2,1,0:T(4,128)S(1)} async-done(((f32[8,4,768]{2,1,0:T(4,128)}), f32[8,4,768]{2,1,0:T(4,128)S(1)}, u32[]{:S(2)}, u32[]{:S(2)}) %all-to-all-start.1) | async-done | bytes 98336 | tf_op jit(solution)/shard_map/all_to_all | solution.py:48
  55.7 3.7 %all-reduce.2 = (bf16[4,6144]{1,0:T(4,128)(2,1)S(1)}, bf16[4,512]{1,0:T(4,128)(2,1)S(1)}) all-reduce(f32[4,6144]{1,0:T(4,128)S(1)} %bitcast.33, f32[4,512]{1,0:T(4,128)S(1)} %all_to_all.50), channel_id=2, replica_groups=mesh['groups'=2,'gx'=8,'yz'=2] {'yz'}, use_global_device_ids=true, to_apply=%region_4.0.clone | all-reduce | flops 26624 | bytes 159744
  59.5 0.0 copy-start.4
  59.6 0.1 fusion.29
  59.7 0.0 copy-done
  59.7 0.8 fusion.42
  60.5 0.2 fusion.7
  60.7 0.4 copy-done.4
  61.1 0.5 fusion.6
  61.6 1.8 %all-gather = bf16[2,2,6144]{2,1,0:T(2,128)(2,1)S(1)} all-gather(bf16[1,2,6144]{2,1,0:T(2,128)(2,1)S(1)} %reshape.57), channel_id=1, replica_groups=mesh['groups'=2,'gx'=8,'yz'=2] {'yz'}, dimensions={0}, use_global_device_ids=true | all-gather | bytes 73728 | tf_op jit(solution)/shard_map/all_gather | solution.py:64
  63.5 0.6 copy.19
  64.1 3.3 %all-to-all-start.3 = ((bf16[4,8,768]{2,0,1:T(4,128)(2,1)}), bf16[4,8,768]{2,0,1:T(4,128)(2,1)S(1)}, u32[]{:S(2)}, u32[]{:S(2)}) async-start(bf16[4,8,768]{2,0,1:T(4,128)(2,1)} %copy.19), calls=%async_computation.3 | async-start | bytes 98304 | tf_op jit(solution)/shard_map/all_to_all | solution.py:65
  67.4 8.9 %fusion.44 = f32[32,1152]{1,0:T(8,128)S(1)} fusion(bf16[32,9216]{1,0:T(8,128)(2,1)S(1)} %reshape.55, bf16[9216,1152]{1,0:T(8,128)(2,1)} %param.12), kind=kOutput, calls=%fused_computation.64 | convolution fusion | flops 679477248 | bytes 21970944 | tf_op jit(solution)/shard_map/dot_general | solution.py:55
  76.3 0.4 collective-permute-start
  76.7 0.0 all-to-all-done.3
  76.7 7.6 %fusion.43 = f32[32,9216]{1,0:T(8,128)S(1)} fusion(bf16[32,768]{1,0:T(8,128)(2,1)S(1)} %all_to_all.54, bf16[768,9216]{1,0:T(8,128)(2,1)} %param.14), kind=kOutput, calls=%fused_computation.63 | convolution fusion | flops 452984832 | bytes 15384576 | tf_op jit(solution)/shard_map/dot_general | solution.py:66
  84.3 0.0 collective-permute-done
  84.3 0.0 copy-start.1
  84.3 10.9 %fusion.2 = bf16[32,9216]{1,0:T(8,128)(2,1)S(1)} fusion(f32[32,9216]{1,0:T(8,128)S(1)} %fusion.43, bf16[1152,9216]{1,0:T(8,128)(2,1)} %param.13, f32[32,1152]{1,0:T(8,128)S(1)} %fusion.44, f32[32,1152]{1,0:T(8,128)S(1)} %collective-permute-done), kind=kOutput, calls=%fused_computation.3 | convolution fusion | flops 680435712 | bytes 23298048 | tf_op jit(solution)/shard_map/dot_general | solution.py:66
  95.2 0.0 copy-start.2
  95.2 0.2 reshape.56
  95.5 22.6 %all_to_all.62 = bf16[8,4,9216]{2,1,0:T(4,128)(2,1)S(1)} all-to-all(bf16[8,4,9216]{2,1,0:T(4,128)(2,1)S(1)} %reshape.56), channel_id=1, replica_groups=mesh['groups'=2,'gx'=8,'yz'=2] {'gx'}, dimensions={0} | all-to-all | bytes 1179648 | tf_op jit(solution)/shard_map/all_to_all | solution.py:70
  118.1 0.2 convert_reduce_fusion
  118.3 0.0 copy-done.2
  118.3 0.7 fusion.23
  119.0 0.0 copy-done.1
  (10 shorter events, 0.2 us)
Async XLA Ops:
  0.0 59.7 %copy-start = (bf16[2,2048,256]{2,1,0:T(8,128)(2,1)S(1)}, bf16[2,2048,256]{2,1,0:T(8,128)(2,1)}, u32[]{:S(2)}) copy-start(bf16[2,2048,256]{2,1,0:T(8,128)(2,1)} %param.15) | copy-start | bytes 6291460
  31.3 11.4 %all-to-all-start.2 = ((f32[8,1,256]{2,1,0:T(1,128)}), f32[8,1,256]{2,1,0:T(1,128)S(1)}, u32[]{:S(2)}, u32[]{:S(2)}) async-start(f32[8,1,256]{2,1,0:T(1,128)} %reshape.67), calls=%async_computation.2 | async-start | bytes 16384 | tf_op jit(solution)/shard_map/all_to_all | solution.py:49
  34.6 14.0 %copy-start.3 = (s32[2]{0:T(128)S(1)}, s32[2]{0:T(128)}, u32[]{:S(2)}) copy-start(s32[2]{0:T(128)} %param.17) | copy-start | bytes 28
  34.6 14.1 %copy-start.5 = (u32[32]{0:T(128)S(1)}, u32[32]{0:T(128)}, u32[]{:S(2)}) copy-start(u32[32]{0:T(128)} %constant.27) | copy-start | bytes 388
  42.7 13.1 %all-to-all-start.1 = ((f32[8,4,768]{2,1,0:T(4,128)}), f32[8,4,768]{2,1,0:T(4,128)S(1)}, u32[]{:S(2)}, u32[]{:S(2)}) async-start(f32[8,4,768]{2,1,0:T(4,128)} %fusion), calls=%async_computation.1 | async-start | bytes 196608 | tf_op jit(solution)/shard_map/all_to_all | solution.py:48
  59.5 1.6 %copy-start.4 = (bf16[2,2048,256]{2,1,0:T(8,128)(2,1)S(1)}, bf16[2,2048,256]{2,1,0:T(8,128)(2,1)}, u32[]{:S(2)}) copy-start(bf16[2,2048,256]{2,1,0:T(8,128)(2,1)} %param.16) | copy-start | bytes 6291460
  64.1 12.6 %all-to-all-start.3 = ((bf16[4,8,768]{2,0,1:T(4,128)(2,1)}), bf16[4,8,768]{2,0,1:T(4,128)(2,1)S(1)}, u32[]{:S(2)}, u32[]{:S(2)}) async-start(bf16[4,8,768]{2,0,1:T(4,128)(2,1)} %copy.19), calls=%async_computation.3 | async-start | bytes 98304 | tf_op jit(solution)/shard_map/all_to_all | solution.py:65
  76.3 8.0 %collective-permute-start = (f32[32,1152]{1,0:T(8,128)S(1)}, f32[32,1152]{1,0:T(8,128)S(1)}, u32[]{:S(2)}, u32[]{:S(2)}) collective-permute-start(f32[32,1152]{1,0:T(8,128)S(1)} %fusion.44), channel_id=1, source_target_pairs={{0,1},{1,0},{2,3},{3,2},{4,5},{5,4},{6,7},{7,6},{8,9},{9,8},{10,11... | collective-permute-start | bytes 442376 | tf_op jit(solution)/shard_map/ppermute | solution.py:56
  84.3 34.7 %copy-start.1 = (bf16[2,2048,256]{2,1,0:T(8,128)(2,1)S(1)}, bf16[2,2048,256]{2,1,0:T(8,128)(2,1)}, u32[]{:S(2)}) copy-start(bf16[2,2048,256]{2,1,0:T(8,128)(2,1)} %param.15) | copy-start | bytes 6291460
  95.2 23.1 %copy-start.2 = (bf16[4,9216]{1,0:T(4,128)(2,1)S(1)}, bf16[4,9216]{1,0:T(4,128)(2,1)}, u32[]{:S(2)}) copy-start(bf16[4,9216]{1,0:T(4,128)(2,1)} %param.9) | copy-start | bytes 221188

commit v2 on v1

--- a/solution.py
+++ b/solution.py
@@ -1,6 +1,10 @@
+import functools
+
 import jax
 import jax.numpy as jnp
 from jax import lax
+from jax.experimental import pallas as pl
+from jax.experimental.pallas import tpu as pltpu
 from jax.sharding import PartitionSpec as P
 
 D = 18432
@@ -70,6 +74,331 @@
     pieces = lax.all_to_all(pieces, "gx", split_axis=0, concat_axis=0, tiled=True)
     branch = jnp.sum(pieces.astype(jnp.float32), axis=0)
     return (x + branch).astype(jnp.bfloat16)
+
+
+def gelu(x):
+    c = 0.7978845608028654
+    return 0.5 * x * (1.0 + jnp.tanh(c * (x + 0.044715 * (x * x * x))))
+
+
+def block_kernel(
+    n, tok, wq, wkv, wi, wo, wa, kc, vc, lens, out,
+    buf_q, buf_i, buf_a, buf_kv, kbuf, vbuf, xf, xb, nbuf, bsend, brecv,
+    mom, mom_in, acc_q, half_in, qsend, qrecv, qs, acc_i, inner_in, hb,
+    asend, arecv, ahalf, ahalf_in,
+    sem_q, sem_i, sem_o, sem_a, sem_l, pair_send, pair_recv, gx_send, gx_recv, b_send, b_recv,
+):
+    g = lax.axis_index("gx")
+    y = lax.axis_index("yz")
+    rows, width = tok.shape
+    half = rows // 2
+    hrows = n * half
+    cq, cols = buf_q.shape[0], buf_q.shape[2]
+    ci, inner = buf_i.shape[0], buf_i.shape[2]
+    per = cols // HEAD
+    groups = b_send.shape[0]
+    wide = width // groups
+
+    def load_q(i):
+        return pltpu.make_async_copy(wq.at[pl.ds(i * cols, cols), :], buf_q.at[i], sem_q.at[i])
+
+    def load_i(i):
+        return pltpu.make_async_copy(wi.at[pl.ds(i * inner, inner), :], buf_i.at[i], sem_i.at[i])
+
+    def load_o(i):
+        return pltpu.make_async_copy(wo.at[:, pl.ds(i * inner, inner)], buf_i.at[i], sem_o.at[i])
+
+    def load_a(i):
+        return pltpu.make_async_copy(wa.at[:, pl.ds(i * cols, cols)], buf_a.at[i], sem_a.at[i])
+
+    load_kv = pltpu.make_async_copy(wkv, buf_kv, sem_l.at[0])
+    load_k = pltpu.make_async_copy(kc, kbuf, sem_l.at[1])
+    load_v = pltpu.make_async_copy(vc, vbuf, sem_l.at[2])
+
+    def each(count, do):
+        def step(i, c):
+            do(i)
+            return c
+
+        lax.fori_loop(0, count, step, 0)
+
+    each(cq, lambda i: load_q(i).start())
+    load_kv.start()
+    each(ci, lambda i: load_i(i).start())
+    load_k.start()
+    load_v.start()
+    each(cq, lambda i: load_a(i).start())
+
+    barrier = pltpu.get_barrier_semaphore()
+    for i in range(1, n):
+        pl.semaphore_signal(
+            barrier, inc=1, device_id={"gx": lax.rem(g + i, n)}, device_id_type=pl.DeviceIdType.MESH
+        )
+    pl.semaphore_signal(barrier, inc=1, device_id={"yz": 1 - y}, device_id_type=pl.DeviceIdType.MESH)
+
+    def to_pair(src, dst, k):
+        return pltpu.make_async_remote_copy(
+            src_ref=src, dst_ref=dst, send_sem=pair_send.at[k], recv_sem=pair_recv.at[k],
+            device_id={"yz": 1 - y}, device_id_type=pl.DeviceIdType.MESH,
+        )
+
+    def to_gx(src, dst, send, recv, i):
+        return pltpu.make_async_remote_copy(
+            src_ref=src, dst_ref=dst, send_sem=send, recv_sem=recv,
+            device_id={"gx": lax.rem(g + i, n)}, device_id_type=pl.DeviceIdType.MESH,
+        )
+
+    x = tok[...].astype(jnp.float32)
+    mom[0:rows, :] = jnp.broadcast_to(jnp.sum(x, axis=1, keepdims=True), (rows, 128))
+    mom[rows : 2 * rows, :] = jnp.broadcast_to(jnp.sum(x * x, axis=1, keepdims=True), (rows, 128))
+    pl.semaphore_wait(barrier, n)
+    exchange = to_pair(mom, mom_in, 0)
+    exchange.start()
+    exchange.wait()
+    both = mom[...] + mom_in[...]
+    mean = both[0:rows, 0:1] / D
+    var = both[rows : 2 * rows, 0:1] / D - mean * mean
+    nbuf[g] = ((x - mean) * lax.rsqrt(var + 1e-05)).astype(jnp.bfloat16)
+
+    gathers = [to_gx(nbuf.at[g], nbuf.at[g], gx_send.at[0, i - 1], gx_recv.at[0, i - 1], i) for i in range(1, n)]
+    for c in gathers:
+        c.start()
+    for c in gathers:
+        c.wait()
+    for s in range(n):
+        v = nbuf[s].astype(jnp.float32)
+        xf[s * half : (s + 1) * half, :] = v[0:half, :]
+        xf[hrows + s * half : hrows + (s + 1) * half, :] = v[half:rows, :]
+    xb[...] = xf[...].astype(jnp.bfloat16)
+
+    acc_q[...] = jnp.zeros_like(acc_q)
+
+    def q_step(i):
+        load_q(i).wait()
+        acc_q[:, 0:cols] += jnp.dot(
+            xb[:, pl.ds(pl.multiple_of(i * cols, 128), cols)], buf_q[i],
+            preferred_element_type=jnp.float32,
+        )
+
+    each(cq, q_step)
+    load_kv.wait()
+    kv = jnp.dot(xb[...], buf_kv[...], preferred_element_type=jnp.float32)
+    kvw = kv.shape[1]
+    spread = 128 // kvw
+    kv = jnp.concatenate([kv] * spread, axis=1)
+    lane = lax.broadcasted_iota(jnp.int32, kv.shape, 1) // kvw
+    acc_q[:, cols : cols + 128] = jnp.where(lane == lax.rem(g, spread), kv, 0.0)
+
+    exchange = to_pair(acc_q.at[pl.ds(pl.multiple_of((1 - y) * hrows, 16), hrows), :], half_in, 1)
+    exchange.start()
+    exchange.wait()
+    mine = acc_q[pl.ds(pl.multiple_of(y * hrows, 16), hrows), :] + half_in[...]
+    mine = mine.astype(jnp.bfloat16).astype(jnp.float32)
+    for s in range(n):
+        qsend[s] = mine[s * half : (s + 1) * half, :]
+    q_copies = [
+        to_gx(qsend.at[lax.rem(g + i, n)], qrecv.at[g], gx_send.at[1, i - 1], gx_recv.at[1, i - 1], i)
+        for i in range(1, n)
+    ]
+    for c in q_copies:
+        c.start()
+    qrecv[g] = qsend[g]
+
+    acc_i[...] = jnp.zeros_like(acc_i)
+
+    def i_step(i):
+        load_i(i).wait()
+        acc_i[...] += jnp.dot(
+            xb[:, pl.ds(pl.multiple_of(i * inner, 128), inner)], buf_i[i],
+            preferred_element_type=jnp.float32,
+        )
+        load_o(i).start()
+
+    each(ci, i_step)
+    inner_copy = to_pair(acc_i, inner_in, 2)
+    inner_copy.start()
+
+    for c in q_copies:
+        c.wait()
+    load_k.wait()
+    load_v.wait()
+    scale = 1.0 / HEAD**0.5
+    for j in range(half):
+        for s in range(n):
+            for h in range(per):
+                qs[j, s * per + h : s * per + h + 1, :] = qrecv[s, j : j + 1, h * HEAD : (h + 1) * HEAD]
+        tails = [qrecv[s, j : j + 1, cols : cols + 128] for s in range(n)]
+        lanes = [sum(tails[t * spread + 1 : (t + 1) * spread], tails[t * spread]) for t in range(n // spread)]
+        new = jnp.concatenate(lanes, axis=1)
+        new_key, new_value = new[:, :HEAD], new[:, HEAD:]
+        q = qs[j]
+        scores = lax.dot_general(
+            q.astype(jnp.bfloat16), kbuf[j], (((1,), (1,)), ((), ())),
+            preferred_element_type=jnp.float32,
+        ) * scale
+        valid = lax.broadcasted_iota(jnp.int32, scores.shape, 1) < lens[j]
+        self_score = jnp.sum(q * new_key, axis=1, keepdims=True) * scale
+        masked = jnp.where(valid, scores, -jnp.inf)
+        top = jnp.maximum(jnp.max(masked, axis=1, keepdims=True), self_score)
+        cached = jnp.where(valid, jnp.exp(masked - top), 0.0)
+        own = jnp.exp(self_score - top)
+        total = jnp.sum(cached, axis=1, keepdims=True) + own
+        weights = (cached / total).astype(jnp.bfloat16)
+        own_w = (own / total).astype(jnp.bfloat16).astype(jnp.float32)
+        res = jnp.dot(weights, vbuf[j], preferred_element_type=jnp.float32) + own_w * new_value
+        res = res.astype(jnp.bfloat16).astype(jnp.float32)
+        for s in range(n):
+            for h in range(per):
+                asend[s, j : j + 1, h * HEAD : (h + 1) * HEAD] = res[s * per + h : s * per + h + 1, :]
+    a_copies = [
+        to_gx(asend.at[lax.rem(g + i, n)], arecv.at[g], gx_send.at[2, i - 1], gx_recv.at[2, i - 1], i)
+        for i in range(1, n)
+    ]
+    for c in a_copies:
+        c.start()
+    arecv[g] = asend[g]
+
+    inner_copy.wait()
+    hb[...] = gelu(acc_i[...] + inner_in[...]).astype(jnp.bfloat16)
+
+    def o_step(i):
+        load_o(i).wait()
+        xf[:, pl.ds(pl.multiple_of(i * inner, 128), inner)] = jnp.dot(
+            hb[...], buf_i[i], preferred_element_type=jnp.float32
+        )
+
+    first = ci // 2
+
+    def o_second(i):
+        o_step(i + first)
+
+    each(first, o_step)
+    for c in a_copies:
+        c.wait()
+    for s in range(n):
+        ahalf[s * half : (s + 1) * half, :] = arecv[s]
+    exchange = to_pair(ahalf, ahalf_in, 3)
+    exchange.start()
+    each(ci - first, o_second)
+    exchange.wait()
+    a_own, a_other = ahalf[...], ahalf_in[...]
+    low = jnp.where(y == 0, a_own, a_other)
+    high = jnp.where(y == 0, a_other, a_own)
+    att = jnp.concatenate([low, high], axis=0).astype(jnp.bfloat16)
+    acc_q[:, 0:cols] = att.astype(jnp.float32)
+
+    def b_copy(k, i):
+        at = pl.ds(pl.multiple_of(k * wide, 128), wide)
+        return to_gx(
+            bsend.at[lax.rem(g + i, n), :, at], brecv.at[g, :, at],
+            b_send.at[k, i - 1], b_recv.at[k, i - 1], i,
+        )
+
+    chunks = wide // cols
+
+    def b_step(k):
+        a = acc_q[:, 0:cols].astype(jnp.bfloat16)
+        for t in range(chunks):
+            m = k * chunks + t
+            load_a(m).wait()
+            at = pl.ds(pl.multiple_of(m * cols, 128), cols)
+            r = xf[:, at] + jnp.dot(a, buf_a[m], preferred_element_type=jnp.float32)
+            for s in range(n):
+                piece = jnp.concatenate(
+                    [r[s * half : (s + 1) * half, :], r[hrows + s * half : hrows + (s + 1) * half, :]],
+                    axis=0,
+                )
+                bsend[s, :, at] = piece.astype(jnp.bfloat16)
+        for i in range(1, n):
+            b_copy(k, i).start()
+
+    each(groups, b_step)
+    brecv[g] = bsend[g]
+
+    def end_step(k):
+        for i in range(1, n):
+            b_copy(k, i).wait()
+        at = pl.ds(pl.multiple_of(k * wide, 128), wide)
+        total = brecv[0, :, at].astype(jnp.float32)
+        for s in range(1, n):
+            total += brecv[s, :, at].astype(jnp.float32)
+        out[:, at] = (tok[:, at].astype(jnp.float32) + total).astype(jnp.bfloat16)
+
+    each(groups, end_step)
+
+
+def fused(n, tokens, w_query, w_keyval, w_inner, w_outer, w_attn_out, key_cache, value_cache, lengths):
+    rows, width = tokens.shape
+    cols, inner, kvw = w_query.shape[1], w_inner.shape[1], w_keyval.shape[1]
+    cq, ci = width // cols, width // inner
+    half = rows // 2
+    all_rows, hrows = n * rows, n * half
+    groups = 4 if cq % 4 == 0 else 1
+    heads = n * cols // HEAD
+    bf, f32 = jnp.bfloat16, jnp.float32
+    V, dma = pltpu.VMEM, pltpu.SemaphoreType.DMA
+    vmem = pl.BlockSpec(memory_space=pltpu.VMEM)
+    hbm = pl.BlockSpec(memory_space=pl.ANY)
+    return pl.pallas_call(
+        functools.partial(block_kernel, n),
+        out_shape=jax.ShapeDtypeStruct(tokens.shape, bf),
+        in_specs=[vmem] + [hbm] * 7 + [pl.BlockSpec(memory_space=pltpu.SMEM)],
+        out_specs=vmem,
+        scratch_shapes=[
+            V((cq, cols, cols), bf),
+            V((ci, inner, inner), bf),
+            V((cq, cols, cols), bf),
+            V((width, kvw), bf),
+            V(key_cache.shape, bf),
+            V(value_cache.shape, bf),
+            V((all_rows, width), f32),
+            V((all_rows, width), bf),
+            V((n, rows, width), bf),
+            V((n, rows, width), bf),
+            V((n, rows, width), bf),
+            V((2 * rows, 128), f32),
+            V((2 * rows, 128), f32),
+            V((all_rows, cols + 128), f32),
+            V((hrows, cols + 128), f32),
+            V((n, half, cols + 128), f32),
+            V((n, half, cols + 128), f32),
+            V((half, heads, HEAD), f32),
+            V((all_rows, inner), f32),
+            V((all_rows, inner), f32),
+            V((all_rows, inner), bf),
+            V((n, half, cols), f32),
+            V((n, half, cols), f32),
+            V((hrows, cols), f32),
+            V((hrows, cols), f32),
+            dma((cq,)),
+            dma((ci,)),
+            dma((ci,)),
+            dma((cq,)),
+            dma((3,)),
+            dma((4,)),
+            dma((4,)),
+            dma((3, n - 1)),
+            dma((3, n - 1)),
+            dma((groups, n - 1)),
+            dma((groups, n - 1)),
+        ],
+        compiler_params=pltpu.CompilerParams(
+            collective_id=0, has_side_effects=True, vmem_limit_bytes=62 * 1024 * 1024
+        ),
+    )(tokens, w_query, w_keyval, w_inner, w_outer, w_attn_out, key_cache, value_cache, lengths)
+
+
+def plan(n):
+    def run(tokens, w_query, w_keyval, w_inner, *rest):
+        width, cols, inner = tokens.shape[1], w_query.shape[1], w_inner.shape[1]
+        fits = (
+            cols % HEAD == 0 and inner % 128 == 0 and width % cols == 0 and width % inner == 0
+            and 128 % w_keyval.shape[1] == 0 and tokens.shape[0] == 4 and n * 2 % 16 == 0
+        )
+        args = (tokens, w_query, w_keyval, w_inner) + rest
+        return fused(n, *args) if fits else body(*args)
+
+    return run
 
 
 def solution(mesh):
@@ -85,4 +414,4 @@
         P(("groups", "gx", "yz")),
     )
     out_specs = P(("groups", "gx"), "yz")
-    return jax.shard_map(body, mesh=mesh, in_specs=in_specs, out_specs=out_specs, check_vma=False)
+    return jax.shard_map(plan(mesh.shape["gx"]), mesh=mesh, in_specs=in_specs, out_specs=out_specs, check_vma=False)

time: 120 us -> 64 us (0.53)
  Pallas kernels: 0 us -> 58.5 us
  blocking collectives: 54.5 us -> 0 us
  matrix products: 38.5 us -> 0 us
  starting transfers between devices: 13 us -> 0 us
  waiting for transfers between devices: 4.3 us -> 0 us
  other arithmetic: 4.17 us -> 0 us
  local copies, waits for them, and re-layouts: 3.63 us -> 5.24 us
    pallas_call x0 -> x1, Pallas kernels: none -> 58.5 us  [fused(): pl.pallas_call(functools.partial(block_kernel, n), out_shape=jax.ShapeDty...]
    all_to_all x2 -> x0, blocking collectives: 46.4 us -> none  [the longest x1 23.8 us: body(): lax.all_to_all(copies, 'gx', split_axis=0, concat_axis=0, tiled=True)]
    dot_general x8 -> x0, matrix products: 38.5 us -> none  [the longest x1 10.9 us: body(): jnp.dot(hidden, w_outer, preferred_element_type=jnp.float32)]
    all_to_all x3 -> x0, starting transfers between devices: 12.6 us -> none  [the longest x1 5.93 us: body(): lax.all_to_all(query_part, 'gx', split_axis=0, concat_axis=1, tiled=True)]
    all_to_all x3 -> x0, waiting for transfers between devices: 4.29 us -> none  [the longest x1 4.29 us: body(): lax.all_to_all(query_part, 'gx', split_axis=0, concat_axis=1, tiled=True)]
    unnamed x1 -> x0, blocking collectives: 3.74 us -> none
    unnamed x16 -> x2, local copies, waits for them, and re-layouts: 1.78 us -> 5.24 us
    psum x1 -> x0, blocking collectives: 2.59 us -> none  [body(): lax.psum((jnp.sum(x, axis=1), jnp.sum(x * x, axis=1)), 'yz')]
  transfers between devices with their start and end apart: 4 -> 0, of which waited for: 1 -> 0; matrix products, arithmetic and copies ran while one was open for 22% -> 0% of each run, Pallas kernels for 0% -> 0%
where the time goes in v2:
time: 64 us; the launch traced here: 63.8 us
  Pallas kernels  58.5 us (91%)
  local copies, waits for them, and re-layouts  5.24 us (8%)
    pallas_call x1, Pallas kernels, fused(): pl.pallas_call(functools.partial(block_kernel, n), out_shape=jax.ShapeDty...  58.5 us
    unnamed x2, local copies, waits for them, and re-layouts  5.24 us

profile of v2, /device:TPU:0, one launch (start us, length us, event | category | flops | bytes accessed | tf_op | source)
XLA Modules:
  0.0 63.8 jit_solution(13500527485303427974)
XLA Ops:
  0.0 3.7 %copy.10.wkv = bf16[9216,64]{1,0:T(8,128)(2,1)} copy(bf16[9216,64]{0,1:T(8,128)(2,1)} %param.11) | data formatting | bytes 2359296 | tf_op args[2]
  3.7 58.5 %shard_map.91 = bf16[4,9216]{1,0:T(4,128)(2,1)} custom-call(bf16[4,9216]{1,0:T(4,128)(2,1)} %tok.1, bf16[9216,768]{1,0:T(8,128)(2,1)} %wq.1, bf16[9216,64]{1,0:T(8,128)(2,1)} %copy.10.wkv, bf16[9216,1152]{1,0:T(8,128)(2,1)} %wi.1, bf16[1152,9216]{1,0:T(8,128)(2,1)} %wo.1, bf16[768,9216]{1,0:T(8,128)(2,1)} %wa.1, bf16[2,2048,256]{2,1,0:T(8,128)(2,1)} %kc.1, ...), custom_call_target="tpu_custom_call" | custom-call | tf_op jit(solution)/shard_map/pallas_call | solution.py:342
  62.2 1.5 %copy.12 = bf16[4,9216]{1,0:T(4,128)(2,1)} copy(bf16[4,9216]{1,0:T(4,128)(2,1)} %shard_map.91) | data formatting | bytes 147456

commit v3 on v2

--- a/solution.py
+++ b/solution.py
@@ -83,13 +83,16 @@
 
 def block_kernel(
     n, tok, wq, wkv, wi, wo, wa, kc, vc, lens, out,
-    buf_q, buf_i, buf_a, buf_kv, kbuf, vbuf, xf, xb, nbuf, bsend, brecv,
+    buf_q, buf_i, buf_a, buf_kv, kbuf, vbuf, xf, xb, nbuf, bsend, xrecv, zsend, zrecv,
     mom, mom_in, acc_q, half_in, qsend, qrecv, qs, acc_i, inner_in, hb,
     asend, arecv, ahalf, ahalf_in,
     sem_q, sem_i, sem_o, sem_a, sem_l, pair_send, pair_recv, gx_send, gx_recv, b_send, b_recv,
 ):
     g = lax.axis_index("gx")
     y = lax.axis_index("yz")
+    zs = n // 2
+    zi, side = lax.div(g, 2), lax.rem(g, 2)
+    beside = zi * 2 + 1 - side
     rows, width = tok.shape
     half = rows // 2
     hrows = n * half
@@ -146,6 +149,12 @@
         return pltpu.make_async_remote_copy(
             src_ref=src, dst_ref=dst, send_sem=send, recv_sem=recv,
             device_id={"gx": lax.rem(g + i, n)}, device_id_type=pl.DeviceIdType.MESH,
+        )
+
+    def to_row(src, dst, send, recv, peer):
+        return pltpu.make_async_remote_copy(
+            src_ref=src, dst_ref=dst, send_sem=send, recv_sem=recv,
+            device_id={"gx": peer}, device_id_type=pl.DeviceIdType.MESH,
         )
 
     x = tok[...].astype(jnp.float32)
@@ -160,11 +169,22 @@
     var = both[rows : 2 * rows, 0:1] / D - mean * mean
     nbuf[g] = ((x - mean) * lax.rsqrt(var + 1e-05)).astype(jnp.bfloat16)
 
-    gathers = [to_gx(nbuf.at[g], nbuf.at[g], gx_send.at[0, i - 1], gx_recv.at[0, i - 1], i) for i in range(1, n)]
-    for c in gathers:
+    def g_copy(slot, m, peer):
+        return to_row(nbuf.at[slot], nbuf.at[slot], gx_send.at[0, m], gx_recv.at[0, m], peer)
+
+    across = g_copy(g, 0, beside)
+    along = [g_copy(g, i, lax.rem(zi + i, zs) * 2 + side) for i in range(1, zs)]
+    onward = [g_copy(lax.rem(zi + zs - i, zs) * 2 + side, zs - 1 + i, beside) for i in range(1, zs)]
+    for c in along:
         c.start()
-    for c in gathers:
-        c.wait()
+    across.start()
+    for c, d in zip(along, onward):
+        c.wait_recv()
+        d.start()
+    across.wait()
+    for c, d in zip(along, onward):
+        c.wait_send()
+        d.wait()
     for s in range(n):
         v = nbuf[s].astype(jnp.float32)
         xf[s * half : (s + 1) * half, :] = v[0:half, :]
@@ -182,7 +202,9 @@
 
     each(cq, q_step)
     load_kv.wait()
-    kv = jnp.dot(xb[...], buf_kv[...], preferred_element_type=jnp.float32)
+    kv = lax.dot_general(
+        xb[...], buf_kv[...], (((1,), (1,)), ((), ())), preferred_element_type=jnp.float32
+    )
     kvw = kv.shape[1]
     spread = 128 // kvw
     kv = jnp.concatenate([kv] * spread, axis=1)
@@ -287,12 +309,29 @@
     att = jnp.concatenate([low, high], axis=0).astype(jnp.bfloat16)
     acc_q[:, 0:cols] = att.astype(jnp.float32)
 
-    def b_copy(k, i):
-        at = pl.ds(pl.multiple_of(k * wide, 128), wide)
-        return to_gx(
-            bsend.at[lax.rem(g + i, n), :, at], brecv.at[g, :, at],
-            b_send.at[k, i - 1], b_recv.at[k, i - 1], i,
-        )
+    def span(k):
+        return pl.ds(k * wide if isinstance(k, int) else pl.multiple_of(k * wide, 128), wide)
+
+    def x_copy(k):
+        return to_row(
+            bsend.at[1 - side, :, :, span(k)], xrecv.at[:, :, span(k)],
+            b_send.at[k, 0], b_recv.at[k, 0], beside,
+        )
+
+    def z_copy(k, i):
+        z = lax.rem(zi + i, zs)
+        return to_row(
+            zsend.at[z, :, span(k)], zrecv.at[zi, :, span(k)],
+            b_send.at[k, i], b_recv.at[k, i], z * 2 + side,
+        )
+
+    def sum_x(k):
+        x_copy(k).wait()
+        for z in range(zs):
+            v = bsend[side, z, :, span(k)].astype(jnp.float32) + xrecv[z, :, span(k)].astype(jnp.float32)
+            zsend[z, :, span(k)] = v.astype(jnp.bfloat16)
+        for i in range(1, zs):
+            z_copy(k, i).start()
 
     chunks = wide // cols
 
@@ -301,27 +340,32 @@
         for t in range(chunks):
             m = k * chunks + t
             load_a(m).wait()
-            at = pl.ds(pl.multiple_of(m * cols, 128), cols)
+            at = pl.ds(m * cols if isinstance(m, int) else pl.multiple_of(m * cols, 128), cols)
             r = xf[:, at] + jnp.dot(a, buf_a[m], preferred_element_type=jnp.float32)
             for s in range(n):
                 piece = jnp.concatenate(
                     [r[s * half : (s + 1) * half, :], r[hrows + s * half : hrows + (s + 1) * half, :]],
                     axis=0,
                 )
-                bsend[s, :, at] = piece.astype(jnp.bfloat16)
-        for i in range(1, n):
-            b_copy(k, i).start()
-
-    each(groups, b_step)
-    brecv[g] = bsend[g]
+                bsend[s % 2, s // 2, :, at] = piece.astype(jnp.bfloat16)
+        x_copy(k).start()
+
+    def b_next(k):
+        b_step(k + 1)
+        sum_x(k)
+
+    b_step(0)
+    each(groups - 1, b_next)
+    sum_x(groups - 1)
+    zrecv[zi] = zsend[zi]
 
     def end_step(k):
-        for i in range(1, n):
-            b_copy(k, i).wait()
-        at = pl.ds(pl.multiple_of(k * wide, 128), wide)
-        total = brecv[0, :, at].astype(jnp.float32)
-        for s in range(1, n):
-            total += brecv[s, :, at].astype(jnp.float32)
+        for i in range(1, zs):
+            z_copy(k, i).wait()
+        at = span(k)
+        total = zrecv[0, :, at].astype(jnp.float32)
+        for z in range(1, zs):
+            total += zrecv[z, :, at].astype(jnp.float32)
         out[:, at] = (tok[:, at].astype(jnp.float32) + total).astype(jnp.bfloat16)
 
     each(groups, end_step)
@@ -348,14 +392,16 @@
             V((cq, cols, cols), bf),
             V((ci, inner, inner), bf),
             V((cq, cols, cols), bf),
-            V((width, kvw), bf),
+            V((kvw, width), bf),
             V(key_cache.shape, bf),
             V(value_cache.shape, bf),
             V((all_rows, width), f32),
             V((all_rows, width), bf),
             V((n, rows, width), bf),
-            V((n, rows, width), bf),
-            V((n, rows, width), bf),
+            V((2, n // 2, rows, width), bf),
+            V((n // 2, rows, width), bf),
+            V((n // 2, rows, width), bf),
+            V((n // 2, rows, width), bf),
             V((2 * rows, 128), f32),
             V((2 * rows, 128), f32),
             V((all_rows, cols + 128), f32),
@@ -379,13 +425,13 @@
             dma((4,)),
             dma((3, n - 1)),
             dma((3, n - 1)),
-            dma((groups, n - 1)),
-            dma((groups, n - 1)),
+            dma((groups, n // 2)),
+            dma((groups, n // 2)),
         ],
         compiler_params=pltpu.CompilerParams(
             collective_id=0, has_side_effects=True, vmem_limit_bytes=62 * 1024 * 1024
         ),
-    )(tokens, w_query, w_keyval, w_inner, w_outer, w_attn_out, key_cache, value_cache, lengths)
+    )(tokens, w_query, w_keyval.T, w_inner, w_outer, w_attn_out, key_cache, value_cache, lengths)
 
 
 def plan(n):

time: 64 us -> 57.1 us (0.89)
  local copies, waits for them, and re-layouts: 5.24 us -> 1.54 us
  Pallas kernels: 58.5 us -> 55.4 us
    unnamed x2 -> x1, local copies, waits for them, and re-layouts: 5.24 us -> 1.54 us
    pallas_call x1, Pallas kernels: 58.5 us -> 55.4 us  [fused(): pl.pallas_call(functools.partial(block_kernel, n), out_shape=jax.ShapeDty...]
where the time goes in v3:
time: 57.1 us; the launch traced here: 56.9 us
  Pallas kernels  55.4 us (97%)
  local copies, waits for them, and re-layouts  1.54 us (3%)
    pallas_call x1, Pallas kernels, fused(): pl.pallas_call(functools.partial(block_kernel, n), out_shape=jax.ShapeDty...  55.4 us
    unnamed x1, local copies, waits for them, and re-layouts  1.54 us

profile of v3, /device:TPU:0, one launch (start us, length us, event | category | flops | bytes accessed | tf_op | source)
XLA Modules:
  0.0 56.9 jit_solution(15731903711291395350)
XLA Ops:
  0.0 55.4 %shard_map.91 = bf16[4,9216]{1,0:T(4,128)(2,1)} custom-call(bf16[4,9216]{1,0:T(4,128)(2,1)} %tok.1, bf16[9216,768]{1,0:T(8,128)(2,1)} %wq.1, bf16[64,9216]{1,0:T(8,128)(2,1)} %bitcast.1, bf16[9216,1152]{1,0:T(8,128)(2,1)} %wi.1, bf16[1152,9216]{1,0:T(8,128)(2,1)} %wo.1, bf16[768,9216]{1,0:T(8,128)(2,1)} %wa.1, bf16[2,2048,256]{2,1,0:T(8,128)(2,1)} %kc.1, ...), custom_call_target="tpu_custom_call" | custom-call | tf_op jit(solution)/shard_map/pallas_call | solution.py:386
  55.4 1.5 %copy.11 = bf16[4,9216]{1,0:T(4,128)(2,1)} copy(bf16[4,9216]{1,0:T(4,128)(2,1)} %shard_map.91) | data formatting | bytes 147456

commit v4 on v3

--- a/solution.py
+++ b/solution.py
@@ -83,10 +83,10 @@
 
 def block_kernel(
     n, tok, wq, wkv, wi, wo, wa, kc, vc, lens, out,
-    buf_q, buf_i, buf_a, buf_kv, kbuf, vbuf, xf, xb, nbuf, bsend, xrecv, zsend, zrecv,
+    buf_q, buf_i, buf_a, buf_kv, kbuf, vbuf, xf, xb, nbuf, bsend, xrecv, zsend, zrecv, own_sum,
     mom, mom_in, acc_q, half_in, qsend, qrecv, qs, acc_i, inner_in, hb,
     asend, arecv, ahalf, ahalf_in,
-    sem_q, sem_i, sem_o, sem_a, sem_l, pair_send, pair_recv, gx_send, gx_recv, b_send, b_recv,
+    sem_q, sem_i, sem_o, sem_a, sem_l, pair_send, pair_recv, gx_send, gx_recv, g_send, g_recv, b_send, b_recv,
 ):
     g = lax.axis_index("gx")
     y = lax.axis_index("yz")
@@ -169,19 +169,26 @@
     var = both[rows : 2 * rows, 0:1] / D - mean * mean
     nbuf[g] = ((x - mean) * lax.rsqrt(var + 1e-05)).astype(jnp.bfloat16)
 
-    def g_copy(slot, m, peer):
-        return to_row(nbuf.at[slot], nbuf.at[slot], gx_send.at[0, m], gx_recv.at[0, m], peer)
-
-    across = g_copy(g, 0, beside)
-    along = [g_copy(g, i, lax.rem(zi + i, zs) * 2 + side) for i in range(1, zs)]
-    onward = [g_copy(lax.rem(zi + zs - i, zs) * 2 + side, zs - 1 + i, beside) for i in range(1, zs)]
-    for c in along:
-        c.start()
-    across.start()
+    def g_copy(k, slot, m, peer):
+        part = nbuf.at[slot, :, k * wide : (k + 1) * wide]
+        return to_row(part, part, g_send.at[k, m], g_recv.at[k, m], peer)
+
+    across = [g_copy(k, g, 0, beside) for k in range(groups)]
+    along, onward = [], []
+    for k in range(groups):
+        along += [g_copy(k, g, i, lax.rem(zi + i, zs) * 2 + side) for i in range(1, zs)]
+        onward += [
+            g_copy(k, lax.rem(zi + zs - i, zs) * 2 + side, zs - 1 + i, beside) for i in range(1, zs)
+        ]
+    for k in range(groups):
+        for c in along[k * (zs - 1) : (k + 1) * (zs - 1)]:
+            c.start()
+        across[k].start()
     for c, d in zip(along, onward):
         c.wait_recv()
         d.start()
-    across.wait()
+    for c in across:
+        c.wait()
     for c, d in zip(along, onward):
         c.wait_send()
         d.wait()
@@ -328,7 +335,8 @@
     def sum_x(k):
         x_copy(k).wait()
         for z in range(zs):
-            v = bsend[side, z, :, span(k)].astype(jnp.float32) + xrecv[z, :, span(k)].astype(jnp.float32)
+            v = own_sum[z, :, span(k)] + xrecv[z, :, span(k)].astype(jnp.float32)
+            own_sum[z, :, span(k)] = v
             zsend[z, :, span(k)] = v.astype(jnp.bfloat16)
         for i in range(1, zs):
             z_copy(k, i).start()
@@ -342,12 +350,16 @@
             load_a(m).wait()
             at = pl.ds(m * cols if isinstance(m, int) else pl.multiple_of(m * cols, 128), cols)
             r = xf[:, at] + jnp.dot(a, buf_a[m], preferred_element_type=jnp.float32)
+            pieces = []
             for s in range(n):
                 piece = jnp.concatenate(
                     [r[s * half : (s + 1) * half, :], r[hrows + s * half : hrows + (s + 1) * half, :]],
                     axis=0,
                 )
                 bsend[s % 2, s // 2, :, at] = piece.astype(jnp.bfloat16)
+                pieces.append(piece)
+            for z in range(zs):
+                own_sum[z, :, at] = jnp.where(side == 0, pieces[2 * z], pieces[2 * z + 1])
         x_copy(k).start()
 
     def b_next(k):
@@ -357,14 +369,14 @@
     b_step(0)
     each(groups - 1, b_next)
     sum_x(groups - 1)
-    zrecv[zi] = zsend[zi]
+    zrecv[zi] = jnp.zeros_like(zrecv[zi])
 
     def end_step(k):
         for i in range(1, zs):
             z_copy(k, i).wait()
         at = span(k)
-        total = zrecv[0, :, at].astype(jnp.float32)
-        for z in range(1, zs):
+        total = own_sum[zi, :, at]
+        for z in range(zs):
             total += zrecv[z, :, at].astype(jnp.float32)
         out[:, at] = (tok[:, at].astype(jnp.float32) + total).astype(jnp.bfloat16)
 
@@ -402,6 +414,7 @@
             V((n // 2, rows, width), bf),
             V((n // 2, rows, width), bf),
             V((n // 2, rows, width), bf),
+            V((n // 2, rows, width), f32),
             V((2 * rows, 128), f32),
             V((2 * rows, 128), f32),
             V((all_rows, cols + 128), f32),
@@ -425,6 +438,8 @@
             dma((4,)),
             dma((3, n - 1)),
             dma((3, n - 1)),
+            dma((groups, n - 1)),
+            dma((groups, n - 1)),
             dma((groups, n // 2)),
             dma((groups, n // 2)),
         ],

time: 57.1 us -> 56.4 us (0.988)
  Pallas kernels: 55.4 us -> 54.6 us
    pallas_call x1, Pallas kernels: 55.4 us -> 54.6 us  [fused(): pl.pallas_call(functools.partial(block_kernel, n), out_shape=jax.ShapeDty...]
where the time goes in v4:
time: 56.4 us; the launch traced here: 56.2 us
  Pallas kernels  54.6 us (97%)
  local copies, waits for them, and re-layouts  1.54 us (3%)
    pallas_call x1, Pallas kernels, fused(): pl.pallas_call(functools.partial(block_kernel, n), out_shape=jax.ShapeDty...  54.6 us
    unnamed x1, local copies, waits for them, and re-layouts  1.54 us

profile of v4, /device:TPU:0, one launch (start us, length us, event | category | flops | bytes accessed | tf_op | source)
XLA Modules:
  0.0 56.2 jit_solution(371990730030655993)
XLA Ops:
  0.0 54.6 %shard_map.91 = bf16[4,9216]{1,0:T(4,128)(2,1)} custom-call(bf16[4,9216]{1,0:T(4,128)(2,1)} %tok.1, bf16[9216,768]{1,0:T(8,128)(2,1)} %wq.1, bf16[64,9216]{1,0:T(8,128)(2,1)} %bitcast.1, bf16[9216,1152]{1,0:T(8,128)(2,1)} %wi.1, bf16[1152,9216]{1,0:T(8,128)(2,1)} %wo.1, bf16[768,9216]{1,0:T(8,128)(2,1)} %wa.1, bf16[2,2048,256]{2,1,0:T(8,128)(2,1)} %kc.1, ...), custom_call_target="tpu_custom_call" | custom-call | tf_op jit(solution)/shard_map/pallas_call | solution.py:398
  54.6 1.5 %copy.11 = bf16[4,9216]{1,0:T(4,128)(2,1)} copy(bf16[4,9216]{1,0:T(4,128)(2,1)} %shard_map.91) | data formatting | bytes 147456
